TPU v7x, 768 devices: a whole 4x8x12 slice. The times are simulated.
768 devices in a mesh: ctx: 96 (over z, x, core), exp: 8 (over y).
Axes of the slice: x: 4, y: 8, z: 12, core: 2. Of those that a mesh axis runs over, the one named last changes fastest.
Arguments:
- ssd_grad: bfloat16 [98304, 4096], P('ctx', 'exp'), may hold values from -6 to 6
- in_proj_b: bfloat16 [98304, 128], P('ctx'), may hold values from -0.1796875 to 0.1796875
- in_proj_c: bfloat16 [98304, 128], P('ctx'), may hold values from -0.1796875 to 0.1796875
- log_decay: float32 [64, 98304], P('exp', 'ctx'), may hold values from -1 to 0
- expert_grad: bfloat16 [98304, 4096], P(('ctx', 'exp')), may hold values from -6 to 6
- route: int32 [98304, 1], P(('ctx', 'exp')), may hold values from 0 to 7; in each aligned block of 128 rows (0 to 127, 128 to 255, ...) at most 24 rows name the same one
- gate_prob: float32 [98304], P(('ctx', 'exp')), may hold values from 0.1 to 1
- down_weight: bfloat16 [8, 768, 4096], P('exp'), may hold values from -0.21875 to 0.21875
- saved_pre: bfloat16 [96, 8, 8, 24, 1536], P('ctx', 'exp'), may hold values from -6 to 6
Outputs:
- input_grad: bfloat16 [98304, 4096], P('ctx', 'exp')
- pre_grad: bfloat16 [96, 8, 8, 24, 1536], P('ctx', 'exp')
Inputs may be any that keep to these rules, and one draw needn't show every extreme that they name: `route`: in each aligned block of 128 rows no expert is named by more than 24 rows.
All inputs are finite; a program needn't handle non-finite values.
Results may differ from a plain program's by a relative error of at most 0.0051.
Values may be sent and summed in bfloat16 or wider, within the bound.
A program may use at most 128 MiB of HBM per device.

v0:
```python
import jax
import jax.numpy as jnp
from jax import lax
from jax.sharding import PartitionSpec as P

BLOCK = 256


def carried_in(value, axis, combine, identity):
    devices, place = (lax.axis_size(axis), lax.axis_index(axis))
    everything = jax.tree.map(lambda part: lax.all_gather(part, axis), value)
    start = jax.tree.map(
        lambda part, zero: jnp.broadcast_to(jnp.asarray(zero, part.dtype), part.shape),
        value,
        identity,
    )

    def lap(k, before):
        at = devices - 1 - k
        reached = at > place
        new = combine(before, jax.tree.map(lambda part: part[at], everything))
        return jax.tree.map(lambda a, b: jnp.where(reached, a, b), new, before)

    return lax.fori_loop(0, devices, lap, start)


def combine_segments(earlier, later):
    return (later[0] * earlier[0], later[1] + later[0][:, None, None] * earlier[1])


def chain_prefix(own_decay, own_sum):
    identity = (jnp.ones_like(own_decay), jnp.zeros_like(own_sum))
    return carried_in((own_decay, own_sum), "ctx", combine_segments, identity)[1]


def within_one(step_input):
    cotangent, b_rows, c_rows, cumulative = step_input
    block_len = b_rows.shape[0]
    scores = jnp.dot(c_rows, b_rows.T, preferred_element_type=jnp.float32)
    log_gap = cumulative[:, :, None] - cumulative[:, None, :]
    causal = jnp.arange(block_len)[:, None] >= jnp.arange(block_len)[None, :]
    weights = jnp.where(
        causal[None], scores[None] * jnp.exp(jnp.minimum(log_gap, 0.0)), 0.0
    ).astype(jnp.bfloat16)
    return jnp.einsum("hts,thp->shp", weights, cotangent, preferred_element_type=jnp.float32)


def fold_block(running, step_input):
    return (step_input[0] + step_input[1][:, None, None] * running, None)


def carry_block(state_grad, step_input):
    updated = step_input[0] + step_input[1][:, None, None] * state_grad
    return (updated, state_grad.astype(jnp.bfloat16))


def expert_side(expert_grad, route, gate_prob, down_weight, saved_pre):
    owners = lax.axis_size("exp")
    capacity = saved_pre.shape[3]
    hidden_units = down_weight.shape[1]
    slot_ids = route[:, 0]
    onehot = (slot_ids[:, None] == jnp.arange(owners, dtype=jnp.int32)[None, :]).astype(jnp.int32)
    before = jnp.cumsum(onehot, axis=0, dtype=jnp.int32) - onehot
    slot_rank = jnp.sum(before * onehot, axis=1, dtype=jnp.int32)
    slot_index = slot_ids * capacity + slot_rank
    placement = (
        slot_index[:, None] == jnp.arange(owners * capacity, dtype=jnp.int32)[None, :]
    ).astype(jnp.bfloat16)
    scaled = (gate_prob[:, None] * expert_grad.astype(jnp.float32)).astype(jnp.bfloat16)
    outgoing = lax.dot_general(
        placement, scaled, (((0,), (0,)), ((), ())), preferred_element_type=jnp.float32
    )
    outgoing = outgoing.astype(jnp.bfloat16).reshape(owners, capacity, expert_grad.shape[1])
    arrived = lax.all_to_all(outgoing, "exp", split_axis=0, concat_axis=0, tiled=True)
    hidden_grad = jnp.einsum(
        "scd,fd->scf", arrived, down_weight[0], preferred_element_type=jnp.float32
    )
    saved_acts = saved_pre[0, 0].astype(jnp.float32)
    gate_pre = saved_acts[..., :hidden_units]
    up_pre = saved_acts[..., hidden_units:]
    sigmoid_gate = jax.nn.sigmoid(gate_pre)
    gate_part = hidden_grad * up_pre * sigmoid_gate * (1.0 + gate_pre * (1.0 - sigmoid_gate))
    up_part = hidden_grad * gate_pre * sigmoid_gate
    return jnp.concatenate([gate_part, up_part], axis=-1).astype(jnp.bfloat16)[None, None]


def body(
    ssd_grad, in_proj_b, in_proj_c, log_decay, expert_grad, route, gate_prob, down_weight, saved_pre
):
    seq_rows = ssd_grad.shape[0]
    heads_here = log_decay.shape[0]
    head_width = ssd_grad.shape[1] // heads_here
    state_size = in_proj_b.shape[1]
    blocks = seq_rows // BLOCK
    cumulative = jnp.cumsum(log_decay.reshape(heads_here, blocks, BLOCK), axis=2)
    block_end = cumulative[:, :, -1]
    block_decay = jnp.exp(block_end)
    cotangent = ssd_grad.reshape(blocks, BLOCK, heads_here, head_width)
    b_block = in_proj_b.reshape(blocks, BLOCK, state_size)
    c_block = in_proj_c.reshape(blocks, BLOCK, state_size)
    weighted_c = (jnp.exp(cumulative)[..., None] * c_block[None].astype(jnp.float32)).astype(
        jnp.bfloat16
    )
    local_state = jnp.einsum(
        "hktn,kthp->khnp", weighted_c, cotangent, preferred_element_type=jnp.float32
    )
    decay_steps = block_decay.T
    zero_state = jnp.zeros((heads_here, state_size, head_width), jnp.float32)
    own_sum, ignored = lax.scan(fold_block, zero_state, (local_state, decay_steps), reverse=True)
    own_decay = jnp.prod(block_decay, axis=1)
    incoming = chain_prefix(own_decay, own_sum)
    within_term = lax.map(
        within_one, (cotangent, b_block, c_block, jnp.transpose(cumulative, (1, 0, 2)))
    )
    leftover, carried = lax.scan(carry_block, incoming, (local_state, decay_steps), reverse=True)
    projected = jnp.einsum("ktn,khnp->kthp", b_block, carried, preferred_element_type=jnp.float32)
    end_weight = jnp.exp(block_end[:, :, None] - cumulative)
    carried_term = projected * jnp.transpose(end_weight, (1, 2, 0))[..., None]
    input_grad = (
        (within_term + carried_term).astype(jnp.bfloat16).reshape(seq_rows, heads_here * head_width)
    )
    pre_grad = expert_side(expert_grad, route, gate_prob, down_weight, saved_pre)
    return (input_grad, pre_grad)


def solution(mesh):
    placed = (
        P("ctx", "exp"),
        P("ctx", None),
        P("ctx", None),
        P("exp", "ctx"),
        P(("ctx", "exp"), None),
        P(("ctx", "exp"), None),
        P(("ctx", "exp")),
        P("exp", None, None),
        P("ctx", "exp", None, None, None),
    )
    return jax.shard_map(
        body,
        mesh=mesh,
        in_specs=placed,
        out_specs=(P("ctx", "exp"), P("ctx", "exp", None, None, None)),
        check_vma=False,
    )
```

profile of v0, /device:TPU:1, one launch (start us, length us, event | category | flops | bytes accessed | tf_op | source)
XLA Modules:
  0.0 406.2 jit_solution(3173844865293732062)
XLA Ops:
  8.0 2.3 reduce-window.6
  10.8 2.8 reshape.124
  13.6 1.9 copy.28
  15.6 3.8 fusion.20
  21.4 3.2 convolution_convert_fusion
  24.6 7.6 %all-to-all-start = ((bf16[8,24,4096]{2,1,0:T(8,128)(2,1)}), bf16[8,24,4096]{2,1,0:T(8,128)(2,1)}, u32[]{:S(2)}, u32[]{:S(2)}) async-start(bf16[8,24,4096]{2,1,0:T(8,128)(2,1)} %bitcast.118), calls=%async_computation | async-start | bytes 3145728 | tf_op jit(solution)/shard_map/all_to_all | solution.py:74
  32.2 1.3 dynamic-slice
  34.4 198.1 %all-reduce = f32[768]{0:T(1024)S(1)} all-reduce(f32[768]{0:T(1024)S(1)} %dynamic-update-slice), channel_id=3, replica_groups=mesh['ctx'=96,'exp'=8] {'ctx'}, use_global_device_ids=true, to_apply=%add | all-reduce | flops 768 | bytes 6144
  232.6 2.2 bitcast_convert_fusion
  234.8 13.9 %while.57 = (s32[]{:T(128)}, f32[4,256,8,64]{1,3,2,0:T(8,128)}, bf16[4,256,8,64]{1,3,2,0:T(8,128)(2,1)}, bf16[4,256,128]{2,1,0:T(8,128)(2,1)S(1)}, bf16[4,256,12...) while((s32[]{:T(128)}, f32[4,256,8,64]{1,3,2,0:T(8,128)}, bf16[4,256,8,64]{1,3,2,0:T(8,128)(2,1)}, ...), condition=%wide.region_3.4_spmd, body=%wide.region_2.3_spmd.sunk | while | flops 86573056 | bytes 1607761 | solution.py:112
  234.8 1.0 fusion.54
  235.9 2.4 fusion.55
  238.3 1.0 fusion.54
  239.4 2.4 fusion.55
  241.8 1.0 fusion.54
  242.9 2.4 fusion.55
  245.3 1.0 fusion.54
  246.4 2.4 fusion.55
  248.7 5.8 %fusion.30 = (bf16[1,1,8,24,768]{4,3,2,1,0:T(8,128)(2,1)S(1)}, bf16[1,1,8,24,768]{4,3,2,1,0:T(8,128)(2,1)S(1)}) fusion(f32[8,24,1536]{2,1,0:T(8,128)} %bitcast_convert_fusion, bf16[8,24,4096]{2,1,0:T(8,128)(2,1)} %all-to-all-done, bf16[1,768,4096]{2,1,0:T(8,128)(2,1)} %param.24), kind=kOutput, calls=%fused_computation.52 | convolution fusion | flops 1209876480 | bytes 9633792 | tf_op jit(solution)/shard_map/scd,fd->scf/dot_general | solution.py:75
  255.4 131.3 %while.60 = (s32[]{:T(128)}, f32[8,128,64]{2,1,0:T(8,128)S(1)}, s32[]{:T(128)}, f32[96,8,128,64]{2,3,1,0:T(8,128)}, f32[96,8]{1,0:T(8,128)S(1)}, /*index=5*/s32[]{:T(128)}, s32[]{:T(128)}, s32[]{:T(128)}, s32[]{:T(128)}) while((s32[]{:T(128)}, f32[8,128,64]{2,1,0:T(8,128)S(1)}, s32[]{:T(128)}, f32[96,8,128,64]{2,3,1,0:T(8,128)}, ...), condition=%wide.region_8.9_spmd.clone, body=%wide.region_7.8_spmd.clone.sunk | while | flops 262152 | bytes 1835271 | solution.py:24
  256.8 1.0 constant_dynamic-slice_fusion.3
  258.2 1.0 constant_dynamic-slice_fusion.3
  259.5 1.0 constant_dynamic-slice_fusion.3
  260.9 1.0 constant_dynamic-slice_fusion.3
  262.3 1.0 constant_dynamic-slice_fusion.3
  263.6 1.0 constant_dynamic-slice_fusion.3
  265.0 1.0 constant_dynamic-slice_fusion.3
  386.8 1.2 broadcast_in_dim.46
  388.0 3.7 while.58
  391.7 3.4 fusion.22
  395.1 2.2 copy.40
  397.3 2.0 reshape.123
  (439 shorter events, 128.2 us)
Async XLA Ops:
  7.2 248.3 %all-gather.4.cloned.1.call-start = ((), (), s32[]{:S(2)}) async-start(), calls=%async_computation.1 | async-start | bytes 25427968 | tf_op jit(solution)/shard_map/all_gather | solution.py:11
  13.6 2.0 copy-start
  19.4 1.6 copy-start.2
  19.4 2.0 copy-start.3
  24.6 224.2 %all-to-all-start = ((bf16[8,24,4096]{2,1,0:T(8,128)(2,1)}), bf16[8,24,4096]{2,1,0:T(8,128)(2,1)}, u32[]{:S(2)}, u32[]{:S(2)}) async-start(bf16[8,24,4096]{2,1,0:T(8,128)(2,1)} %bitcast.118), calls=%async_computation | async-start | bytes 3145728 | tf_op jit(solution)/shard_map/all_to_all | solution.py:74
  388.0 3.7 copy-start.1
Sparse Core Ops, SparseCore 0:
  21.1 163.7 all-gather.3
where the time goes:
time: 413 us; the launch traced here: 406 us
  blocking collectives  198 us (48%)
  local copies, waits for them, and re-layouts  128 us (31%)
  matrix products  29.9 us (7%)
  other arithmetic  22.6 us (5%)
  between operations  14.9 us (4%)
  starting transfers between devices  7.69 us (2%)
  loops' own time  5.43 us (1%)
    unnamed x1, blocking collectives  198 us
    dynamic_slice x192, local copies, waits for them, and re-layouts, lap(): new = combine(before, jax.tree.map(lambda part: part[at], everything))  113 us
    select_n x96, other arithmetic, lap(): return jax.tree.map(lambda a, b: jnp.where(reached, a, b), new, before)  12.4 us
    dot_general x4, matrix products, within_one(): jnp.einsum('hts,thp->shp', weights, cotangent, preferred_element_type=jnp...  9.58 us
  transfers between devices with their start and end apart: 2, of which 0 were waited for; matrix products, arithmetic and copies ran while one was open for 7% of the time, Pallas kernels for 0%

commit v1 on v0

v1 whole, which is shorter than its diff:
```python
import functools
import math

import jax
import jax.numpy as jnp
from jax import lax
from jax.experimental import pallas as pl
from jax.experimental.pallas import tpu as pltpu
from jax.sharding import PartitionSpec as P

MESH = pl.DeviceIdType.MESH
F32, BF16 = jnp.float32, jnp.bfloat16
BLOCK = 256
PLANE = 8
CHUNKS = 8
LOG2E = math.log2(math.e)
EXTRA = 8
NT = (((1,), (1,)), ((), ()))


def mm(a, b):
    return jnp.dot(a, b, preferred_element_type=F32)


def mm_nt(a, b, precision=None):
    return lax.dot_general(a, b, NT, preferred_element_type=F32, precision=precision)


def iota(shape, dim):
    return lax.broadcasted_iota(jnp.int32, shape, dim)


def decay_rows(d):
    return jnp.broadcast_to(d, (EXTRA, d.shape[1]))


def kernel(
    sizes,
    g_hbm, b_hbm, c_hbm, ld_hbm, x_hbm, route_hbm, gate_hbm, w_hbm, saved_hbm,
    ig_hbm, pg_hbm,
    g, b, c, ld, x, route, gate, w, saved,
    snd, rcv, st1, ph1, st2, ph2, st3, ph3,
    cum, cumt, ls, within, endw, hid, fac_g, fac_u, ig, pg,
    load_sem, out_sem, ss, rs, ss1, rs1, ss2, rs2, ss3, rs3,
):
    n_exp, n_z, heads, width, blocks, cap, ff = sizes
    state = b.shape[1]
    ctx, y = lax.axis_index("ctx"), lax.axis_index("exp")
    z, p = ctx // PLANE, lax.rem(ctx, PLANE)

    def load(i, src, dst):
        copy = pltpu.make_async_copy(src, dst, load_sem.at[i])
        copy.start()
        return copy

    l_route = load(0, route_hbm, route)
    l_gate = load(1, gate_hbm, gate)
    l_x = load(2, x_hbm, x)

    barrier = pltpu.get_barrier_semaphore()

    def greet(device):
        pl.semaphore_signal(barrier, inc=1, device_id=device, device_id_type=MESH)

    for d in (4, 3, 5, 2, 6, 1, 7):
        greet((ctx, lax.rem(y + d, n_exp)))

    def greet_higher(at, carry):
        greet((at * PLANE + p, y))
        return carry

    lax.fori_loop(z + 1, n_z, greet_higher, 0)
    for d in range(1, PLANE):
        greet((z * PLANE + lax.rem(p + d, PLANE), y))

    l_ld = load(3, ld_hbm, ld)
    l_c = load(4, c_hbm, c)
    l_g = load(5, g_hbm, g)
    l_b = load(6, b_hbm, b)
    l_w = load(7, w_hbm, w)
    l_saved = load(8, saved_hbm, saved)

    rows = x.shape[0]
    slots = n_exp * cap
    l_route.wait()
    l_gate.wait()
    which = route[...]
    onehot = jnp.where(iota((n_exp, rows), 0) == which, 1.0, 0.0)
    earlier = jnp.where(iota((rows, rows), 0) < iota((rows, rows), 1), 1.0, 0.0).astype(BF16)
    before = mm(onehot.astype(BF16), earlier)
    rank = jnp.sum(before * onehot, axis=0, keepdims=True)
    slot = which * cap + rank.astype(jnp.int32)
    here = iota((slots, rows), 0) == slot
    slot_gate = jnp.sum(jnp.where(here, gate[...], 0.0), axis=1, keepdims=True)
    pick = jnp.where(here, 1.0, 0.0).astype(BF16)
    chunk = x.shape[1] // CHUNKS
    half = chunk // 2
    l_x.wait()

    def pack(i):
        part = mm(pick, x[:, i * chunk:(i + 1) * chunk]) * slot_gate
        for e in range(n_exp):
            mine = part[e * cap:(e + 1) * cap]
            both = jnp.concatenate([mine[:, :half], mine[:, half:]], axis=0)
            snd[i, e] = both.astype(BF16)

    for i in range(CHUNKS):
        pack(i)

    pl.semaphore_wait(barrier, n_exp - 1 + PLANE - 1 + z)

    def row_copy(i, d):
        to = lax.rem(y + d, n_exp)
        return pltpu.make_async_remote_copy(
            src_ref=snd.at[i, to], dst_ref=rcv.at[i, y],
            send_sem=ss.at[i, d], recv_sem=rs.at[i, d],
            device_id=(ctx, to), device_id_type=MESH,
        )

    for i in range(CHUNKS):
        for d in (4, 3, 5, 2, 6, 1, 7):
            row_copy(i, d).start()

    l_ld.wait()
    up = jnp.where(iota((BLOCK, BLOCK), 0) <= iota((BLOCK, BLOCK), 1), 1.0, 0.0)
    down = jnp.where(iota((BLOCK, BLOCK), 1) <= iota((BLOCK, BLOCK), 0), 1.0, 0.0)
    for k in range(blocks):
        steps = ld[:, k * BLOCK:(k + 1) * BLOCK]
        cum[k] = jnp.dot(steps, up, preferred_element_type=F32, precision=lax.Precision.HIGHEST)
        cumt[k] = mm_nt(down, steps, precision=lax.Precision.HIGHEST)

    columns = heads * width
    own_lane = iota((heads, columns), 1) // width == iota((heads, columns), 0)

    def spread(column):
        wide = jnp.where(own_lane, jnp.broadcast_to(column, (heads, columns)), 0.0)
        return jnp.sum(wide, axis=0, keepdims=True)

    decay = [jnp.exp(cum[k][:, BLOCK - 1:BLOCK]) for k in range(blocks)]
    decay_row = [spread(d) for d in decay]

    group = 256
    per = group // width
    lane_head = iota((BLOCK, group), 1) // width

    def own_columns(part):
        return jnp.concatenate(
            [jnp.where(lane_head == j, part, jnp.zeros_like(part)) for j in range(per)], axis=0
        )

    l_c.wait()
    l_g.wait()
    eye = jnp.where(iota((state, state), 0) == iota((state, state), 1), 1.0, 0.0).astype(BF16)

    def local(k, carry):
        at = pl.multiple_of(k * BLOCK, BLOCK)
        ct = mm_nt(eye, c[pl.ds(at, BLOCK), :])
        grown = jnp.exp(cum[k])
        for q in range(heads // per):
            left = jnp.concatenate(
                [(ct * grown[q * per + j:q * per + j + 1, :]).astype(BF16) for j in range(per)],
                axis=1,
            )
            right = own_columns(g[pl.ds(at, BLOCK), q * group:(q + 1) * group])
            ls[k, :, q * group:(q + 1) * group] = mm(left, right)
        return carry

    lax.fori_loop(0, blocks, local, 0)

    total = ls[blocks - 1]
    for k in reversed(range(blocks - 1)):
        total = ls[k] + decay_row[k] * total
    whole_decay = decay[0]
    for k in range(1, blocks):
        whole_decay = whole_decay * decay[k]
    total_t = total.T
    wide_decay = jnp.broadcast_to(whole_decay, (heads, state))
    for h in range(heads):
        st1[h, :width, :] = total_t[h * width:(h + 1) * width, :]
        st1[h, width:, :] = decay_rows(wide_decay[h:h + 1, :])

    def plane_copy(src, dst, s_sem, r_sem, d):
        to = lax.rem(p + d, PLANE)
        return pltpu.make_async_remote_copy(
            src_ref=src.at[to], dst_ref=dst.at[p],
            send_sem=s_sem.at[d], recv_sem=r_sem.at[d],
            device_id=(z * PLANE + to, y), device_id_type=MESH,
        )

    for d in range(1, PLANE):
        plane_copy(st1, ph1, ss1, rs1, d).start()
    ph1[p] = st1[p]

    l_b.wait()
    later = iota((BLOCK, BLOCK), 1) >= iota((BLOCK, BLOCK), 0)

    def inside(k, carry):
        at = pl.multiple_of(k * BLOCK, BLOCK)
        scores = mm_nt(b[pl.ds(at, BLOCK), :], c[pl.ds(at, BLOCK), :])
        scores = jnp.where(later, scores, 0.0)
        across = cum[k] * LOG2E
        along = cumt[k] * LOG2E
        for q in range(heads // per):
            parts = []
            for j in range(per):
                h = q * per + j
                gap = jnp.minimum(across[h:h + 1, :] - along[:, h:h + 1], 0.0)
                parts.append((scores * jnp.exp2(gap)).astype(BF16))
            left = jnp.concatenate(parts, axis=1)
            right = own_columns(g[pl.ds(at, BLOCK), q * group:(q + 1) * group])
            within[pl.ds(at, BLOCK), q * group:(q + 1) * group] = mm(left, right)
        rest = jnp.exp2(along[BLOCK - 1:BLOCK, :] - along)
        first = iota((BLOCK, 2 * width), 1) < width
        for q in range(heads // 2):
            endw[pl.ds(at, BLOCK), q * 2 * width:(q + 1) * 2 * width] = jnp.where(
                first, rest[:, 2 * q:2 * q + 1], rest[:, 2 * q + 1:2 * q + 2]
            )
        return carry

    lax.fori_loop(0, blocks // 2, inside, 0)

    for d in range(1, PLANE):
        plane_copy(st1, ph1, ss1, rs1, d).wait_recv()

    def parts_of(ref, at):
        return (
            ref[at, :width, :],
            ref[at, width:width + 1, :],
        )

    plane_sum, plane_decay = parts_of(ph1, PLANE - 1)
    for i in reversed(range(PLANE - 1)):
        s, d = parts_of(ph1, i)
        plane_sum = s + d * plane_sum
        plane_decay = plane_decay * d
    st2[:width, :] = plane_sum
    st2[width:, :] = decay_rows(plane_decay)

    def z_copy(to, at):
        return pltpu.make_async_remote_copy(
            src_ref=st2, dst_ref=ph2.at[at],
            send_sem=ss2.at[to], recv_sem=rs2.at[at],
            device_id=(to * PLANE + p, y), device_id_type=MESH,
        )

    def send_lower(to, carry):
        z_copy(to, z).start()
        return carry

    lax.fori_loop(0, z, send_lower, 0)

    lax.fori_loop(blocks // 2, blocks, inside, 0)

    l_saved.wait()

    def factors(s, carry):
        pre = saved[s].astype(F32)
        gate_pre, up_pre = pre[:, :ff], pre[:, ff:]
        sig = 1.0 / (1.0 + jnp.exp(-gate_pre))
        fac_g[s] = up_pre * sig * (1.0 + gate_pre * (1.0 - sig))
        fac_u[s] = gate_pre * sig
        return carry

    lax.fori_loop(0, n_exp, factors, 0)

    l_w.wait()

    def expert(i):
        rcv[i, y] = snd[i, y]
        for d in range(1, n_exp):
            row_copy(i, d).wait_recv()
        got = [rcv[i, s].astype(F32) for s in range(n_exp)]
        left = jnp.concatenate([m[:cap] for m in got], axis=0)
        right = jnp.concatenate([m[cap:] for m in got], axis=0)
        arrived = jnp.concatenate([left, right], axis=1).astype(BF16)
        part = mm_nt(arrived, w[:, i * chunk:(i + 1) * chunk])
        if i == 0:
            hid[...] = part
        elif i < CHUNKS - 1:
            hid[...] += part
        else:
            part = hid[...] + part
            for s in range(n_exp):
                mine = part[s * cap:(s + 1) * cap]
                pg[s, :, :ff] = (mine * fac_g[s]).astype(BF16)
                pg[s, :, ff:] = (mine * fac_u[s]).astype(BF16)

    expert(0)
    expert(1)

    def from_higher(j, incoming):
        at = n_z - 1 - j
        z_copy(0, at).wait_recv()
        s, d = parts_of(ph2, at)
        return s + d * incoming

    incoming = lax.fori_loop(0, n_z - 1 - z, from_higher, jnp.zeros((width, state), F32))
    for i in reversed(range(PLANE)):
        st3[i] = incoming
        if i > 0:
            s, d = parts_of(ph1, i)
            incoming = s + d * incoming
    for d in range(1, PLANE):
        plane_copy(st3, ph3, ss3, rs3, d).start()
    ph3[p] = st3[p]

    expert(2)
    expert(3)

    for d in range(1, PLANE):
        plane_copy(st3, ph3, ss3, rs3, d).wait_recv()
    carried = jnp.concatenate([ph3[h] for h in range(heads)], axis=0).T
    stores = []
    for k in reversed(range(blocks)):
        here = slice(k * BLOCK, (k + 1) * BLOCK)
        projected = mm(b[here, :], carried.astype(BF16))
        ig[here, :] = (within[here, :] + projected * endw[here, :]).astype(BF16)
        store = pltpu.make_async_copy(ig.at[here], ig_hbm.at[here], out_sem.at[k])
        store.start()
        stores.append(store)
        if k > 0:
            carried = ls[k] + decay_row[k] * carried

    for i in range(4, CHUNKS):
        expert(i)
    store = pltpu.make_async_copy(pg, pg_hbm, out_sem.at[blocks])
    store.start()
    stores.append(store)

    for i in range(CHUNKS):
        for d in range(1, n_exp):
            row_copy(i, d).wait_send()
    for d in range(1, PLANE):
        plane_copy(st1, ph1, ss1, rs1, d).wait_send()
        plane_copy(st3, ph3, ss3, rs3, d).wait_send()

    def sent_lower(to, carry):
        z_copy(to, z).wait_send()
        return carry

    lax.fori_loop(0, z, sent_lower, 0)
    for store in stores:
        store.wait()


def body(
    ssd_grad, in_proj_b, in_proj_c, log_decay, expert_grad, route, gate_prob, down_weight, saved_pre
):
    n_exp, n_z = lax.axis_size("exp"), lax.axis_size("ctx") // PLANE
    rows_seq, columns = ssd_grad.shape
    heads = log_decay.shape[0]
    width = columns // heads
    blocks = rows_seq // BLOCK
    state = in_proj_b.shape[1]
    rows, d_model = expert_grad.shape
    cap, ff = saved_pre.shape[3], down_weight.shape[1]
    half = d_model // CHUNKS // 2
    sizes = (n_exp, n_z, heads, width, blocks, cap, ff)
    dma = pltpu.SemaphoreType.DMA
    vmem = pltpu.VMEM
    scratch = [
        vmem((rows_seq, columns), BF16), vmem((rows_seq, state), BF16), vmem((rows_seq, state), BF16),
        vmem((heads, rows_seq), F32), vmem((rows, d_model), BF16), vmem((1, rows), jnp.int32),
        vmem((1, rows), F32), vmem((ff, d_model), BF16), vmem((n_exp, cap, 2 * ff), BF16),
        vmem((CHUNKS, n_exp, 2 * cap, half), BF16), vmem((CHUNKS, n_exp, 2 * cap, half), BF16),
        vmem((PLANE, width + EXTRA, state), F32), vmem((PLANE, width + EXTRA, state), F32),
        vmem((width + EXTRA, state), F32), vmem((n_z, width + EXTRA, state), F32),
        vmem((PLANE, width, state), F32), vmem((PLANE, width, state), F32),
        vmem((blocks, heads, BLOCK), F32), vmem((blocks, BLOCK, heads), F32),
        vmem((blocks, state, columns), F32), vmem((rows_seq, columns), F32),
        vmem((rows_seq, columns), F32), vmem((n_exp * cap, ff), F32),
        vmem((n_exp, cap, ff), F32), vmem((n_exp, cap, ff), F32),
        vmem((rows_seq, columns), BF16), vmem((n_exp, cap, 2 * ff), BF16),
        dma((9,)), dma((blocks + 1,)), dma((CHUNKS, n_exp)), dma((CHUNKS, n_exp)),
        dma((PLANE,)), dma((PLANE,)), dma((n_z,)), dma((n_z,)), dma((PLANE,)), dma((PLANE,)),
    ]
    any_space = pl.BlockSpec(memory_space=pl.ANY)
    input_grad, pre_grad = pl.pallas_call(
        functools.partial(kernel, sizes),
        out_shape=(
            jax.ShapeDtypeStruct((rows_seq, columns), BF16),
            jax.ShapeDtypeStruct((n_exp, cap, 2 * ff), BF16),
        ),
        in_specs=[any_space] * 9,
        out_specs=(any_space, any_space),
        scratch_shapes=scratch,
        compiler_params=pltpu.CompilerParams(
            collective_id=0, has_side_effects=True, vmem_limit_bytes=56 * 2**20
        ),
        name="hybrid",
    )(
        ssd_grad, in_proj_b, in_proj_c, log_decay, expert_grad,
        route.reshape(1, rows), gate_prob.reshape(1, rows), down_weight[0], saved_pre[0, 0],
    )
    return input_grad, pre_grad[None, None]


def solution(mesh):
    placed = (
        P("ctx", "exp"),
        P("ctx", None),
        P("ctx", None),
        P("exp", "ctx"),
        P(("ctx", "exp"), None),
        P(("ctx", "exp"), None),
        P(("ctx", "exp")),
        P("exp", None, None),
        P("ctx", "exp", None, None, None),
    )
    return jax.shard_map(
        body,
        mesh=mesh,
        in_specs=placed,
        out_specs=(P("ctx", "exp"), P("ctx", "exp", None, None, None)),
        check_vma=False,
    )
```

time: 413 us -> 57.4 us (0.14); the launches traced: 406 us -> 57.2 us
  blocking collectives: 198 us -> 0 us
  local copies, waits for them, and re-layouts: 128 us -> 4.18 us
  Pallas kernels: 0 us -> 52.4 us
  matrix products: 29.9 us -> 0 us
  other arithmetic: 22.6 us -> 0 us
  between operations: 14.9 us -> 0.64 us
  starting transfers between devices: 7.69 us -> 0 us
  loops' own time: 5.43 us -> 0 us
    unnamed x1 -> x0, blocking collectives: 198 us -> none
    dynamic_slice x192 -> x0, local copies, waits for them, and re-layouts: 113 us -> none  [lap(): new = combine(before, jax.tree.map(lambda part: part[at], everything))]
    pallas_call x0 -> x1, Pallas kernels: none -> 52.4 us  [body(): pl.pallas_call(functools.partial(kernel, sizes), out_shape=(jax.ShapeDtyp...]
    dot_general x12 -> x0, matrix products: 29.9 us -> none  [the longest x4 9.58 us: within_one(): jnp.einsum('hts,thp->shp', weights, cotangent, preferred_element_type=jnp...]
    select_n x96 -> x0, other arithmetic: 12.4 us -> none  [lap(): return jax.tree.map(lambda a, b: jnp.where(reached, a, b), new, before)]
    all_to_all x1 -> x0, starting transfers between devices: 7.65 us -> none  [expert_side(): lax.all_to_all(outgoing, 'exp', split_axis=0, concat_axis=0, tiled=True)]
    another operation x4 -> x0, loops' own time: 5.43 us -> none  [the longest x1 5.13 us: carried_in(): return lax.fori_loop(0, devices, lap, start)]
  transfers between devices with their start and end apart: 2 -> 0, of which waited for: 0 -> 0; matrix products, arithmetic and copies ran while one was open for 7% -> 0% of each run, Pallas kernels for 0% -> 0%
where the time goes in v1:
time: 57.4 us; the launch traced here: 57.2 us
  Pallas kernels  52.4 us (91%)
  local copies, waits for them, and re-layouts  4.18 us (7%)
  between operations  0.64 us (1%)
    pallas_call x1, Pallas kernels, body(): pl.pallas_call(functools.partial(kernel, sizes), out_shape=(jax.ShapeDtyp...  52.4 us
    unnamed x2, local copies, waits for them, and re-layouts  4.18 us

profile of v1, /device:TPU:1, one launch (start us, length us, event | category | flops | bytes accessed | tf_op | source)
XLA Modules:
  0.0 57.2 jit_solution(3068031908739562107)
XLA Ops:
  0.6 52.4 %hybrid.1 = (bf16[1024,512]{1,0:T(8,128)(2,1)}, bf16[8,24,1536]{2,1,0:T(8,128)(2,1)}) custom-call(bf16[1024,512]{1,0:T(8,128)(2,1)} %g_hbm.1, bf16[1024,128]{1,0:T(8,128)(2,1)} %b_hbm.1, bf16[1024,128]{1,0:T(8,128)(2,1)} %c_hbm.1, f32[8,1024]{1,0:T(8,128)} %ld_hbm.1, bf16[128,4096]{1,0:T(8,128)(2,1)} %x_hbm.1, s32[1,128]{1,0:T(1,128)} %bitcast.8, ...), custom_call_target="tpu_custom_call" | custom-call | tf_op jit(solution)/shard_map/hybrid/pallas_call | solution.py:378
  53.0 2.3 %copy.13 = bf16[1024,512]{1,0:T(8,128)(2,1)} copy(bf16[1024,512]{1,0:T(8,128)(2,1)} %get-tuple-element.8) | data formatting | bytes 2097152
  55.3 1.9 %copy.14 = bf16[1,1,8,24,1536]{4,3,2,1,0:T(8,128)(2,1)} copy(bf16[1,1,8,24,1536]{4,3,2,1,0:T(8,128)(2,1)} %bitcast.7) | data formatting | bytes 1179648

commit v2 on v1

--- a/solution.py
+++ b/solution.py
@@ -9,12 +9,13 @@
 from jax.sharding import PartitionSpec as P
 
 MESH = pl.DeviceIdType.MESH
-F32, BF16 = jnp.float32, jnp.bfloat16
+F32, BF16, I16 = jnp.float32, jnp.bfloat16, jnp.int16
 BLOCK = 256
 PLANE = 8
-CHUNKS = 8
+Z_GROUP = 3
+CHUNKS = 4
 LOG2E = math.log2(math.e)
-EXTRA = 8
+EXTRA, EXTRA16, ONE16 = 8, 16, 14
 NT = (((1,), (1,)), ((), ()))
 
 
@@ -32,6 +33,25 @@
 
 def decay_rows(d):
     return jnp.broadcast_to(d, (EXTRA, d.shape[1]))
+
+
+def to_fixed(value, d):
+    top = jnp.max(jnp.abs(value), axis=(0, 1), keepdims=True)
+    power = jnp.ceil(jnp.log2(jnp.maximum(top, 1e-30)))
+    power = jnp.broadcast_to(power, (1, value.shape[1]))
+    coded = jnp.round(value * jnp.exp2(ONE16 - power))
+    high = jnp.floor(d * 2.0**ONE16)
+    low = jnp.round((d * 2.0**ONE16 - high) * 2.0**ONE16)
+    row = iota((EXTRA16, value.shape[1]), 0)
+    rows = jnp.where(row == 0, power, jnp.where(row == 1, high, low))
+    return jnp.concatenate([coded, rows], axis=0).astype(jnp.int32).astype(jnp.int16)
+
+
+def from_fixed(coded, width):
+    wide = coded.astype(jnp.int32).astype(F32)
+    rows = wide[width:width + 8]
+    value = wide[:width] * jnp.exp2(rows[0:1] - ONE16)
+    return value, (rows[1:2] + rows[2:3] * 2.0**-ONE16) * 2.0**-ONE16
 
 
 def kernel(
@@ -39,9 +59,9 @@
     g_hbm, b_hbm, c_hbm, ld_hbm, x_hbm, route_hbm, gate_hbm, w_hbm, saved_hbm,
     ig_hbm, pg_hbm,
     g, b, c, ld, x, route, gate, w, saved,
-    snd, rcv, st1, ph1, st2, ph2, st3, ph3,
+    snd, rcv, st1, ph1, st2, ph2, st3, ph3, st4, ph4,
     cum, cumt, ls, within, endw, hid, fac_g, fac_u, ig, pg,
-    load_sem, out_sem, ss, rs, ss1, rs1, ss2, rs2, ss3, rs3,
+    load_sem, out_sem, ss, rs, ss1, rs1, ss2, rs2, ss3, rs3, ss4, rs4,
 ):
     n_exp, n_z, heads, width, blocks, cap, ff = sizes
     state = b.shape[1]
@@ -65,11 +85,22 @@
     for d in (4, 3, 5, 2, 6, 1, 7):
         greet((ctx, lax.rem(y + d, n_exp)))
 
-    def greet_higher(at, carry):
+    in_group = lax.rem(z, Z_GROUP)
+    first = z - in_group
+    group_at = z // Z_GROUP
+    group_end = jnp.minimum(first + Z_GROUP, n_z)
+    groups = -(-n_z // Z_GROUP)
+
+    def greet_plane(at, carry):
         greet((at * PLANE + p, y))
         return carry
 
-    lax.fori_loop(z + 1, n_z, greet_higher, 0)
+    def greet_group(at, carry):
+        greet((at * Z_GROUP * PLANE + p, y))
+        return carry
+
+    lax.fori_loop(z + 1, group_end, greet_plane, 0)
+    lax.fori_loop(group_at + 1, groups, greet_group, 0)
     for d in range(1, PLANE):
         greet((z * PLANE + lax.rem(p + d, PLANE), y))
 
@@ -107,8 +138,6 @@
     for i in range(CHUNKS):
         pack(i)
 
-    pl.semaphore_wait(barrier, n_exp - 1 + PLANE - 1 + z)
-
     def row_copy(i, d):
         to = lax.rem(y + d, n_exp)
         return pltpu.make_async_remote_copy(
@@ -116,10 +145,6 @@
             send_sem=ss.at[i, d], recv_sem=rs.at[i, d],
             device_id=(ctx, to), device_id_type=MESH,
         )
-
-    for i in range(CHUNKS):
-        for d in (4, 3, 5, 2, 6, 1, 7):
-            row_copy(i, d).start()
 
     l_ld.wait()
     up = jnp.where(iota((BLOCK, BLOCK), 0) <= iota((BLOCK, BLOCK), 1), 1.0, 0.0)
@@ -147,6 +172,13 @@
         return jnp.concatenate(
             [jnp.where(lane_head == j, part, jnp.zeros_like(part)) for j in range(per)], axis=0
         )
+
+    lower = jnp.where(in_group == 0, z, 0)
+    pl.semaphore_wait(barrier, n_exp - 1 + PLANE - 1 + in_group + lower)
+
+    for i in range(CHUNKS):
+        for d in (4, 3, 5, 2, 6, 1, 7):
+            row_copy(i, d).start()
 
     l_c.wait()
     l_g.wait()
@@ -169,7 +201,9 @@
 
     total = ls[blocks - 1]
     for k in reversed(range(blocks - 1)):
-        total = ls[k] + decay_row[k] * total
+        inner = total
+        total = ls[k] + decay_row[k] * inner
+        ls[k] = inner
     whole_decay = decay[0]
     for k in range(1, blocks):
         whole_decay = whole_decay * decay[k]
@@ -217,7 +251,7 @@
             )
         return carry
 
-    lax.fori_loop(0, blocks // 2, inside, 0)
+    lax.fori_loop(0, blocks, inside, 0)
 
     for d in range(1, PLANE):
         plane_copy(st1, ph1, ss1, rs1, d).wait_recv()
@@ -243,13 +277,38 @@
             device_id=(to * PLANE + p, y), device_id_type=MESH,
         )
 
-    def send_lower(to, carry):
+    def group_copy(to, at):
+        return pltpu.make_async_remote_copy(
+            src_ref=st4, dst_ref=ph4.at[at],
+            send_sem=ss4.at[to], recv_sem=rs4.at[at],
+            device_id=(to * PLANE + p, y), device_id_type=MESH,
+        )
+
+    def send_plane(to, carry):
         z_copy(to, z).start()
         return carry
 
-    lax.fori_loop(0, z, send_lower, 0)
-
-    lax.fori_loop(blocks // 2, blocks, inside, 0)
+    def send_group(to, carry):
+        group_copy(to, group_at).start()
+        return carry
+
+    lax.fori_loop(first, z, send_plane, 0)
+
+    def from_plane(at, carry):
+        incoming, reach = carry
+        z_copy(0, at).wait_recv()
+        s, d = parts_of(ph2, at)
+        return incoming + reach * s, reach * d
+
+    none = (jnp.zeros((width, state), F32), jnp.ones((1, state), F32))
+    later_planes = lax.fori_loop(z + 1, group_end, from_plane, none)
+
+    @pl.when(in_group == 0)
+    def _():
+        st4[...] = to_fixed(
+            plane_sum + plane_decay * later_planes[0], plane_decay * later_planes[1]
+        )
+        lax.fori_loop(0, first, send_group, 0)
 
     l_saved.wait()
 
@@ -285,16 +344,13 @@
                 pg[s, :, :ff] = (mine * fac_g[s]).astype(BF16)
                 pg[s, :, ff:] = (mine * fac_u[s]).astype(BF16)
 
-    expert(0)
-    expert(1)
-
-    def from_higher(j, incoming):
-        at = n_z - 1 - j
-        z_copy(0, at).wait_recv()
-        s, d = parts_of(ph2, at)
-        return s + d * incoming
-
-    incoming = lax.fori_loop(0, n_z - 1 - z, from_higher, jnp.zeros((width, state), F32))
+    def from_group(at, carry):
+        incoming, reach = carry
+        group_copy(0, at).wait_recv()
+        s, d = from_fixed(ph4[at], width)
+        return incoming + reach * s, reach * d
+
+    incoming = lax.fori_loop(group_at + 1, groups, from_group, later_planes)[0]
     for i in reversed(range(PLANE)):
         st3[i] = incoming
         if i > 0:
@@ -304,24 +360,27 @@
         plane_copy(st3, ph3, ss3, rs3, d).start()
     ph3[p] = st3[p]
 
-    expert(2)
-    expert(3)
+    expert(0)
 
     for d in range(1, PLANE):
         plane_copy(st3, ph3, ss3, rs3, d).wait_recv()
-    carried = jnp.concatenate([ph3[h] for h in range(heads)], axis=0).T
+    incoming = jnp.concatenate([ph3[h] for h in range(heads)], axis=0).T
     stores = []
+    reach = None
     for k in reversed(range(blocks)):
         here = slice(k * BLOCK, (k + 1) * BLOCK)
+        if reach is None:
+            carried = incoming
+        else:
+            carried = ls[k] + reach * incoming
+        reach = decay_row[k] if reach is None else reach * decay_row[k]
         projected = mm(b[here, :], carried.astype(BF16))
         ig[here, :] = (within[here, :] + projected * endw[here, :]).astype(BF16)
         store = pltpu.make_async_copy(ig.at[here], ig_hbm.at[here], out_sem.at[k])
         store.start()
         stores.append(store)
-        if k > 0:
-            carried = ls[k] + decay_row[k] * carried
-
-    for i in range(4, CHUNKS):
+
+    for i in range(1, CHUNKS):
         expert(i)
     store = pltpu.make_async_copy(pg, pg_hbm, out_sem.at[blocks])
     store.start()
@@ -334,11 +393,16 @@
         plane_copy(st1, ph1, ss1, rs1, d).wait_send()
         plane_copy(st3, ph3, ss3, rs3, d).wait_send()
 
-    def sent_lower(to, carry):
+    def sent_plane(to, carry):
         z_copy(to, z).wait_send()
         return carry
 
-    lax.fori_loop(0, z, sent_lower, 0)
+    def sent_group(to, carry):
+        group_copy(to, group_at).wait_send()
+        return carry
+
+    lax.fori_loop(first, z, sent_plane, 0)
+    lax.fori_loop(0, lower, sent_group, 0)
     for store in stores:
         store.wait()
 
@@ -366,6 +430,7 @@
         vmem((PLANE, width + EXTRA, state), F32), vmem((PLANE, width + EXTRA, state), F32),
         vmem((width + EXTRA, state), F32), vmem((n_z, width + EXTRA, state), F32),
         vmem((PLANE, width, state), F32), vmem((PLANE, width, state), F32),
+        vmem((width + EXTRA16, state), I16), vmem((n_z, width + EXTRA16, state), I16),
         vmem((blocks, heads, BLOCK), F32), vmem((blocks, BLOCK, heads), F32),
         vmem((blocks, state, columns), F32), vmem((rows_seq, columns), F32),
         vmem((rows_seq, columns), F32), vmem((n_exp * cap, ff), F32),
@@ -373,6 +438,7 @@
         vmem((rows_seq, columns), BF16), vmem((n_exp, cap, 2 * ff), BF16),
         dma((9,)), dma((blocks + 1,)), dma((CHUNKS, n_exp)), dma((CHUNKS, n_exp)),
         dma((PLANE,)), dma((PLANE,)), dma((n_z,)), dma((n_z,)), dma((PLANE,)), dma((PLANE,)),
+        dma((n_z,)), dma((n_z,)),
     ]
     any_space = pl.BlockSpec(memory_space=pl.ANY)
     input_grad, pre_grad = pl.pallas_call(
@@ -381,16 +447,21 @@
             jax.ShapeDtypeStruct((rows_seq, columns), BF16),
             jax.ShapeDtypeStruct((n_exp, cap, 2 * ff), BF16),
         ),
-        in_specs=[any_space] * 9,
+        in_specs=[pl.BlockSpec(memory_space=pltpu.HBM)] * 9,
         out_specs=(any_space, any_space),
         scratch_shapes=scratch,
         compiler_params=pltpu.CompilerParams(
-            collective_id=0, has_side_effects=True, vmem_limit_bytes=56 * 2**20
+            collective_id=0, has_side_effects=True, vmem_limit_bytes=40 * 2**20
         ),
         name="hybrid",
     )(
-        ssd_grad, in_proj_b, in_proj_c, log_decay, expert_grad,
-        route.reshape(1, rows), gate_prob.reshape(1, rows), down_weight[0], saved_pre[0, 0],
+        *[
+            pltpu.with_memory_space_constraint(operand, pltpu.HBM)
+            for operand in (
+                ssd_grad, in_proj_b, in_proj_c, log_decay, expert_grad, route.reshape(1, rows),
+                gate_prob.reshape(1, rows), down_weight[0], saved_pre[0, 0],
+            )
+        ]
     )
     return input_grad, pre_grad[None, None]
 

time: 57.4 us -> 48.3 us (0.84)
  Pallas kernels: 52.4 us -> 45.6 us
  local copies, waits for them, and re-layouts: 4.18 us -> 1.79 us
    pallas_call x1, Pallas kernels: 52.4 us -> 45.6 us  [body(): pl.pallas_call(functools.partial(kernel, sizes), out_shape=(jax.ShapeDtyp...]
    unnamed x2, local copies, waits for them, and re-layouts: 4.18 us -> 1.79 us
where the time goes in v2:
time: 48.3 us; the launch traced here: 48.1 us
  Pallas kernels  45.6 us (94%)
  local copies, waits for them, and re-layouts  1.79 us (4%)
  between operations  0.64 us (1%)
    pallas_call x1, Pallas kernels, body(): pl.pallas_call(functools.partial(kernel, sizes), out_shape=(jax.ShapeDtyp...  45.6 us
    unnamed x2, local copies, waits for them, and re-layouts  1.79 us

profile of v2, /device:TPU:1, one launch (start us, length us, event | category | flops | bytes accessed | tf_op | source)
XLA Modules:
  0.0 48.1 jit_solution(14996201065941097031)
XLA Ops:
  0.6 45.6 %hybrid.1 = (bf16[1024,512]{1,0:T(8,128)(2,1)S(1)}, bf16[8,24,1536]{2,1,0:T(8,128)(2,1)S(1)}) custom-call(bf16[1024,512]{1,0:T(8,128)(2,1)} %g_hbm.1, bf16[1024,128]{1,0:T(8,128)(2,1)} %b_hbm.1, bf16[1024,128]{1,0:T(8,128)(2,1)} %c_hbm.1, f32[8,1024]{1,0:T(8,128)} %ld_hbm.1, bf16[128,4096]{1,0:T(8,128)(2,1)} %x_hbm.1, s32[1,128]{1,0:T(1,128)} %bitcast.8, ...), custom_call_target="tpu_custom_call" | custom-call | tf_op jit(solution)/shard_map/hybrid/pallas_call | solution.py:444
  46.3 1.0 %copy.13 = bf16[1024,512]{1,0:T(8,128)(2,1)} copy(bf16[1024,512]{1,0:T(8,128)(2,1)S(1)} %get-tuple-element.8) | data formatting | bytes 2097152
  47.2 0.8 %copy.14 = bf16[1,1,8,24,1536]{4,3,2,1,0:T(8,128)(2,1)} copy(bf16[1,1,8,24,1536]{4,3,2,1,0:T(8,128)(2,1)S(1)} %bitcast.5) | data formatting | bytes 1179648

commit v3 on v2

--- a/solution.py
+++ b/solution.py
@@ -57,11 +57,11 @@
 def kernel(
     sizes,
     g_hbm, b_hbm, c_hbm, ld_hbm, x_hbm, route_hbm, gate_hbm, w_hbm, saved_hbm,
-    ig_hbm, pg_hbm,
+    ig, pg,
     g, b, c, ld, x, route, gate, w, saved,
     snd, rcv, st1, ph1, st2, ph2, st3, ph3, st4, ph4,
-    cum, cumt, ls, within, endw, hid, fac_g, fac_u, ig, pg,
-    load_sem, out_sem, ss, rs, ss1, rs1, ss2, rs2, ss3, rs3, ss4, rs4,
+    cum, cumt, ls, within, endw, hid, fac_g, fac_u,
+    load_sem, ss, rs, ss1, rs1, ss2, rs2, ss3, rs3, ss4, rs4,
 ):
     n_exp, n_z, heads, width, blocks, cap, ff = sizes
     state = b.shape[1]
@@ -73,17 +73,22 @@
         copy.start()
         return copy
 
+    barrier = pltpu.get_barrier_semaphore()
+
+    def greet(device):
+        pl.semaphore_signal(barrier, inc=1, device_id=device, device_id_type=MESH)
+
+    for d in (4, 3, 5, 2, 6, 1, 7):
+        greet((ctx, lax.rem(y + d, n_exp)))
+
     l_route = load(0, route_hbm, route)
     l_gate = load(1, gate_hbm, gate)
-    l_x = load(2, x_hbm, x)
-
-    barrier = pltpu.get_barrier_semaphore()
-
-    def greet(device):
-        pl.semaphore_signal(barrier, inc=1, device_id=device, device_id_type=MESH)
-
-    for d in (4, 3, 5, 2, 6, 1, 7):
-        greet((ctx, lax.rem(y + d, n_exp)))
+    chunk = x.shape[1] // CHUNKS
+    half = chunk // 2
+    l_x = []
+    for i in range(CHUNKS):
+        here = slice(i * chunk, (i + 1) * chunk)
+        l_x.append(load(9 + i, x_hbm.at[:, here], x.at[:, here]))
 
     in_group = lax.rem(z, Z_GROUP)
     first = z - in_group
@@ -124,19 +129,14 @@
     here = iota((slots, rows), 0) == slot
     slot_gate = jnp.sum(jnp.where(here, gate[...], 0.0), axis=1, keepdims=True)
     pick = jnp.where(here, 1.0, 0.0).astype(BF16)
-    chunk = x.shape[1] // CHUNKS
-    half = chunk // 2
-    l_x.wait()
 
     def pack(i):
+        l_x[i].wait()
         part = mm(pick, x[:, i * chunk:(i + 1) * chunk]) * slot_gate
         for e in range(n_exp):
             mine = part[e * cap:(e + 1) * cap]
             both = jnp.concatenate([mine[:, :half], mine[:, half:]], axis=0)
             snd[i, e] = both.astype(BF16)
-
-    for i in range(CHUNKS):
-        pack(i)
 
     def row_copy(i, d):
         to = lax.rem(y + d, n_exp)
@@ -146,6 +146,7 @@
             device_id=(ctx, to), device_id_type=MESH,
         )
 
+    pack(0)
     l_ld.wait()
     up = jnp.where(iota((BLOCK, BLOCK), 0) <= iota((BLOCK, BLOCK), 1), 1.0, 0.0)
     down = jnp.where(iota((BLOCK, BLOCK), 1) <= iota((BLOCK, BLOCK), 0), 1.0, 0.0)
@@ -154,6 +155,14 @@
         cum[k] = jnp.dot(steps, up, preferred_element_type=F32, precision=lax.Precision.HIGHEST)
         cumt[k] = mm_nt(down, steps, precision=lax.Precision.HIGHEST)
 
+    lower = jnp.where(in_group == 0, z, 0)
+    pl.semaphore_wait(barrier, n_exp - 1 + PLANE - 1 + in_group + lower)
+    for i in range(CHUNKS):
+        if i > 0:
+            pack(i)
+        for d in (4, 3, 5, 2, 6, 1, 7):
+            row_copy(i, d).start()
+
     columns = heads * width
     own_lane = iota((heads, columns), 1) // width == iota((heads, columns), 0)
 
@@ -172,13 +181,6 @@
         return jnp.concatenate(
             [jnp.where(lane_head == j, part, jnp.zeros_like(part)) for j in range(per)], axis=0
         )
-
-    lower = jnp.where(in_group == 0, z, 0)
-    pl.semaphore_wait(barrier, n_exp - 1 + PLANE - 1 + in_group + lower)
-
-    for i in range(CHUNKS):
-        for d in (4, 3, 5, 2, 6, 1, 7):
-            row_copy(i, d).start()
 
     l_c.wait()
     l_g.wait()
@@ -360,12 +362,12 @@
         plane_copy(st3, ph3, ss3, rs3, d).start()
     ph3[p] = st3[p]
 
-    expert(0)
+    for i in range(CHUNKS - 1):
+        expert(i)
 
     for d in range(1, PLANE):
         plane_copy(st3, ph3, ss3, rs3, d).wait_recv()
     incoming = jnp.concatenate([ph3[h] for h in range(heads)], axis=0).T
-    stores = []
     reach = None
     for k in reversed(range(blocks)):
         here = slice(k * BLOCK, (k + 1) * BLOCK)
@@ -376,15 +378,8 @@
         reach = decay_row[k] if reach is None else reach * decay_row[k]
         projected = mm(b[here, :], carried.astype(BF16))
         ig[here, :] = (within[here, :] + projected * endw[here, :]).astype(BF16)
-        store = pltpu.make_async_copy(ig.at[here], ig_hbm.at[here], out_sem.at[k])
-        store.start()
-        stores.append(store)
-
-    for i in range(1, CHUNKS):
-        expert(i)
-    store = pltpu.make_async_copy(pg, pg_hbm, out_sem.at[blocks])
-    store.start()
-    stores.append(store)
+
+    expert(CHUNKS - 1)
 
     for i in range(CHUNKS):
         for d in range(1, n_exp):
@@ -403,8 +398,6 @@
 
     lax.fori_loop(first, z, sent_plane, 0)
     lax.fori_loop(0, lower, sent_group, 0)
-    for store in stores:
-        store.wait()
 
 
 def body(
@@ -435,12 +428,10 @@
         vmem((blocks, state, columns), F32), vmem((rows_seq, columns), F32),
         vmem((rows_seq, columns), F32), vmem((n_exp * cap, ff), F32),
         vmem((n_exp, cap, ff), F32), vmem((n_exp, cap, ff), F32),
-        vmem((rows_seq, columns), BF16), vmem((n_exp, cap, 2 * ff), BF16),
-        dma((9,)), dma((blocks + 1,)), dma((CHUNKS, n_exp)), dma((CHUNKS, n_exp)),
+        dma((9 + CHUNKS,)), dma((CHUNKS, n_exp)), dma((CHUNKS, n_exp)),
         dma((PLANE,)), dma((PLANE,)), dma((n_z,)), dma((n_z,)), dma((PLANE,)), dma((PLANE,)),
         dma((n_z,)), dma((n_z,)),
     ]
-    any_space = pl.BlockSpec(memory_space=pl.ANY)
     input_grad, pre_grad = pl.pallas_call(
         functools.partial(kernel, sizes),
         out_shape=(
@@ -448,7 +439,7 @@
             jax.ShapeDtypeStruct((n_exp, cap, 2 * ff), BF16),
         ),
         in_specs=[pl.BlockSpec(memory_space=pltpu.HBM)] * 9,
-        out_specs=(any_space, any_space),
+        out_specs=(pl.BlockSpec(memory_space=pltpu.VMEM),) * 2,
         scratch_shapes=scratch,
         compiler_params=pltpu.CompilerParams(
             collective_id=0, has_side_effects=True, vmem_limit_bytes=40 * 2**20

time: 48.3 us -> 48.2 us (level); the launches traced: 48.1 us -> 47.2 us
  Pallas kernels: 45.6 us -> 44.8 us
    pallas_call x1, Pallas kernels: 45.6 us -> 44.8 us  [body(): pl.pallas_call(functools.partial(kernel, sizes), out_shape=(jax.ShapeDtyp...]
where the time goes in v3:
time: 48.2 us; the launch traced here: 47.2 us
  Pallas kernels  44.8 us (93%)
  local copies, waits for them, and re-layouts  1.79 us (4%)
  between operations  0.64 us (1%)
    pallas_call x1, Pallas kernels, body(): pl.pallas_call(functools.partial(kernel, sizes), out_shape=(jax.ShapeDtyp...  44.8 us
    unnamed x2, local copies, waits for them, and re-layouts  1.79 us

profile of v3, /device:TPU:1, one launch (start us, length us, event | category | flops | bytes accessed | tf_op | source)
XLA Modules:
  0.0 47.2 jit_solution(3460287975857767999)
XLA Ops:
  0.6 44.8 %hybrid.1 = (bf16[1024,512]{1,0:T(8,128)(2,1)S(1)}, bf16[8,24,1536]{2,1,0:T(8,128)(2,1)S(1)}) custom-call(bf16[1024,512]{1,0:T(8,128)(2,1)} %g_hbm.1, bf16[1024,128]{1,0:T(8,128)(2,1)} %b_hbm.1, bf16[1024,128]{1,0:T(8,128)(2,1)} %c_hbm.1, f32[8,1024]{1,0:T(8,128)} %ld_hbm.1, bf16[128,4096]{1,0:T(8,128)(2,1)} %x_hbm.1, s32[1,128]{1,0:T(1,128)} %bitcast.8, ...), custom_call_target="tpu_custom_call" | custom-call | tf_op jit(solution)/shard_map/hybrid/pallas_call | solution.py:435
  45.4 1.0 %copy.13 = bf16[1024,512]{1,0:T(8,128)(2,1)} copy(bf16[1024,512]{1,0:T(8,128)(2,1)S(1)} %get-tuple-element.8) | data formatting | bytes 2097152
  46.4 0.8 %copy.14 = bf16[1,1,8,24,1536]{4,3,2,1,0:T(8,128)(2,1)} copy(bf16[1,1,8,24,1536]{4,3,2,1,0:T(8,128)(2,1)S(1)} %bitcast.5) | data formatting | bytes 1179648

commit v4 on v3

--- a/solution.py
+++ b/solution.py
@@ -13,6 +13,7 @@
 BLOCK = 256
 PLANE = 8
 Z_GROUP = 3
+ROW_ORDER = (4, 3, 5, 2, 6, 1, 7)
 CHUNKS = 4
 LOG2E = math.log2(math.e)
 EXTRA, EXTRA16, ONE16 = 8, 16, 14
@@ -61,7 +62,7 @@
     g, b, c, ld, x, route, gate, w, saved,
     snd, rcv, st1, ph1, st2, ph2, st3, ph3, st4, ph4,
     cum, cumt, ls, within, endw, hid, fac_g, fac_u,
-    load_sem, ss, rs, ss1, rs1, ss2, rs2, ss3, rs3, ss4, rs4,
+    load_sem, ss, rs, ss1, rs1, ss2, rs2, ss3, rs3, ss4, rs4, known,
 ):
     n_exp, n_z, heads, width, blocks, cap, ff = sizes
     state = b.shape[1]
@@ -78,8 +79,14 @@
     def greet(device):
         pl.semaphore_signal(barrier, inc=1, device_id=device, device_id_type=MESH)
 
-    for d in (4, 3, 5, 2, 6, 1, 7):
-        greet((ctx, lax.rem(y + d, n_exp)))
+    speaks_later = (ctx == 0) & (y == 0)
+    sends_later = (ctx == 0) & (y > 0)
+
+    @pl.when(jnp.logical_not(speaks_later))
+    def _():
+        for d in ROW_ORDER:
+            greet((ctx, lax.rem(y + d, n_exp)))
+
 
     l_route = load(0, route_hbm, route)
     l_gate = load(1, gate_hbm, gate)
@@ -156,12 +163,32 @@
         cumt[k] = mm_nt(down, steps, precision=lax.Precision.HIGHEST)
 
     lower = jnp.where(in_group == 0, z, 0)
-    pl.semaphore_wait(barrier, n_exp - 1 + PLANE - 1 + in_group + lower)
+    ring = jnp.where(sends_later, n_exp - 2, n_exp - 1)
+    pl.semaphore_wait(barrier, ring + PLANE - 1 + in_group + lower)
+
+    @pl.when(speaks_later)
+    def _():
+        for d in ROW_ORDER:
+            to = lax.rem(y + d, n_exp)
+            pl.semaphore_signal(known, inc=1, device_id=(ctx, to), device_id_type=MESH)
+
+    def send_rows(i):
+        @pl.when(jnp.logical_not(sends_later))
+        def _():
+            for d in ROW_ORDER:
+                row_copy(i, d).start()
+
+        @pl.when(sends_later)
+        def _():
+            for d in ROW_ORDER:
+                @pl.when(lax.rem(y + d, n_exp) > 0)
+                def _():
+                    row_copy(i, d).start()
+
     for i in range(CHUNKS):
         if i > 0:
             pack(i)
-        for d in (4, 3, 5, 2, 6, 1, 7):
-            row_copy(i, d).start()
+        send_rows(i)
 
     columns = heads * width
     own_lane = iota((heads, columns), 1) // width == iota((heads, columns), 0)
@@ -254,6 +281,12 @@
         return carry
 
     lax.fori_loop(0, blocks, inside, 0)
+
+    @pl.when(sends_later)
+    def _():
+        pl.semaphore_wait(known, 1)
+        for i in range(CHUNKS):
+            row_copy(i, n_exp - y).start()
 
     for d in range(1, PLANE):
         plane_copy(st1, ph1, ss1, rs1, d).wait_recv()
@@ -430,7 +463,7 @@
         vmem((n_exp, cap, ff), F32), vmem((n_exp, cap, ff), F32),
         dma((9 + CHUNKS,)), dma((CHUNKS, n_exp)), dma((CHUNKS, n_exp)),
         dma((PLANE,)), dma((PLANE,)), dma((n_z,)), dma((n_z,)), dma((PLANE,)), dma((PLANE,)),
-        dma((n_z,)), dma((n_z,)),
+        dma((n_z,)), dma((n_z,)), pltpu.SemaphoreType.REGULAR,
     ]
     input_grad, pre_grad = pl.pallas_call(
         functools.partial(kernel, sizes),

time: 48.2 us -> 47.5 us (0.985); the launches traced: 47.2 us -> 47.3 us
  no operation moved by 1% of the time
where the time goes in v4:
time: 47.5 us; the launch traced here: 47.3 us
  Pallas kernels  44.8 us (94%)
  local copies, waits for them, and re-layouts  1.79 us (4%)
  between operations  0.64 us (1%)
    pallas_call x1, Pallas kernels, body(): pl.pallas_call(functools.partial(kernel, sizes), out_shape=(jax.ShapeDtyp...  44.8 us
    unnamed x2, local copies, waits for them, and re-layouts  1.79 us

profile of v4, /device:TPU:1, one launch (start us, length us, event | category | flops | bytes accessed | tf_op | source)
XLA Modules:
  0.0 47.3 jit_solution(9836640612513873348)
XLA Ops:
  0.6 44.8 %hybrid.1 = (bf16[1024,512]{1,0:T(8,128)(2,1)S(1)}, bf16[8,24,1536]{2,1,0:T(8,128)(2,1)S(1)}) custom-call(bf16[1024,512]{1,0:T(8,128)(2,1)} %g_hbm.1, bf16[1024,128]{1,0:T(8,128)(2,1)} %b_hbm.1, bf16[1024,128]{1,0:T(8,128)(2,1)} %c_hbm.1, f32[8,1024]{1,0:T(8,128)} %ld_hbm.1, bf16[128,4096]{1,0:T(8,128)(2,1)} %x_hbm.1, s32[1,128]{1,0:T(1,128)} %bitcast.8, ...), custom_call_target="tpu_custom_call" | custom-call | tf_op jit(solution)/shard_map/hybrid/pallas_call | solution.py:468
  45.5 1.0 %copy.13 = bf16[1024,512]{1,0:T(8,128)(2,1)} copy(bf16[1024,512]{1,0:T(8,128)(2,1)S(1)} %get-tuple-element.8) | data formatting | bytes 2097152
  46.4 0.8 %copy.14 = bf16[1,1,8,24,1536]{4,3,2,1,0:T(8,128)(2,1)} copy(bf16[1,1,8,24,1536]{4,3,2,1,0:T(8,128)(2,1)S(1)} %bitcast.5) | data formatting | bytes 1179648
